TPU v7x, 32 devices: a whole 2x2x4 slice. The times are simulated.
32 devices in a mesh: case: 2 (over y), wall: 4 (over z), azim: 4 (over x, core).
Axes of the slice: x: 2, y: 2, z: 4, core: 2. Of those that a mesh axis runs over, the one named last changes fastest.
Arguments:
- state: float32 [12, 2, 32, 512], P(None, 'case', 'wall', 'azim'), parts along dimension 1, may hold values from 0.5 to 1.5
- courant: float32 [2, 32, 512], P('case', 'wall', 'azim'), parts along dimension 0, may hold values from -0.6 to 0.6
- cross_sections: float32 [64], replicated, may hold values from 0.02 to 0.6
- band_fractions: float32 [64], replicated, may hold values from 0.02 to 0.2
- absorb_index: int32 [11, 16], replicated, may hold values from 0 to 63
- band_index: int32 [16], replicated, may hold values from 0 to 63
Outputs:
- new_state: float32 [12, 2, 32, 512], P(None, 'case', 'wall', 'azim'), parts along dimension 1
- wall_flux: float32 [2, 512], P('case', 'azim'), parts along dimension 0
There are 2 independent parts, one for each index of `case`. A program takes and returns all parts, laid end to end along the dimension named above; an argument that names none is the same for every part. Nothing has to cross between parts.
All inputs are finite; a program needn't handle non-finite values.
Results may differ from a plain program's by a relative error of at most 0.0003.
Values sent between devices are 32-bit elements; how exact they have to be, the bound alone decides.
A program may use at most 64 MiB of HBM per device.

v0:
```python
import jax
import jax.numpy as jnp
from jax import lax
from jax.sharding import PartitionSpec as P

KERNEL_WEIGHTS = (0.55, 0.45)
KERNEL_RATES = (1.15, 3.4)
FILTER_STRENGTH = 0.02
COUPLING = 0.1


def with_halo(block, sides, width):
    for axis, dim in sides:
        count = lax.axis_size(axis)
        forward = [(i, i + 1) for i in range(count - 1)]
        forward.append((count - 1, 0))
        backward = [(target, source) for source, target in forward]
        low = lax.ppermute(
            lax.slice_in_dim(block, block.shape[dim] - width, None, axis=dim), axis, forward
        )
        high = lax.ppermute(lax.slice_in_dim(block, 0, width, axis=dim), axis, backward)
        block = jnp.concatenate([low, block, high], axis=dim)
    return block


def band_tables(absorb_index, band_index, cross_sections, band_fractions):
    entries = cross_sections.shape[0]
    table_slots = lax.broadcasted_iota(jnp.int32, (1, 1, entries), 2)
    spectral_absorber_area = jnp.sum(
        jnp.where(absorb_index[:, :, None] == table_slots, cross_sections[None, None, :], 0.0),
        axis=2,
    )
    chosen_values = jnp.where(band_index[:, None] == table_slots[0], band_fractions[None, :], 0.0)
    return (spectral_absorber_area, jnp.sum(chosen_values, axis=1))


def viewing_line_irradiance(
    kinetic_heat_level,
    species_concentrations,
    spectral_absorber_area,
    spectral_fraction_weight,
    mesh_cell_width,
    viewing_line_dimension,
):
    absorption = jnp.einsum(
        "kb,kij->bij",
        spectral_absorber_area,
        species_concentrations,
        precision=lax.Precision.HIGHEST,
    )
    optical_thickness_step = absorption * mesh_cell_width
    optical_depth = (
        lax.cumsum(optical_thickness_step, viewing_line_dimension) - 0.5 * optical_thickness_step
    )
    radiated_energy_rate = (
        spectral_fraction_weight[:, None, None]
        * kinetic_heat_level[None] ** 4
        * optical_thickness_step
    )
    net_flux = 0.0
    wall_flux = 0.0
    for weight, decay_rate in zip(KERNEL_WEIGHTS, KERNEL_RATES):
        growth = jnp.exp(decay_rate * optical_depth)
        falloff = jnp.exp(-decay_rate * optical_depth)
        upward = falloff * lax.cumsum(radiated_energy_rate * growth, viewing_line_dimension)
        tail_sum = lax.cumsum(radiated_energy_rate * falloff, viewing_line_dimension, reverse=True)
        net_flux = net_flux + weight * jnp.sum(upward - growth * tail_sum, axis=0)
        wall_flux = wall_flux + weight * jnp.sum(
            lax.index_in_dim(tail_sum, 0, viewing_line_dimension, keepdims=False), axis=0
        )
    return (net_flux, wall_flux)


def edge_pad(net_flux, viewing_line_dimension):
    count = net_flux.shape[viewing_line_dimension]
    first_row = lax.slice_in_dim(net_flux, 0, 1, axis=viewing_line_dimension)
    last_row = lax.slice_in_dim(net_flux, count - 1, count, axis=viewing_line_dimension)
    return jnp.concatenate([first_row, net_flux, last_row], viewing_line_dimension)


def divergence(padded, viewing_line_dimension, mesh_cell_width):
    count = padded.shape[viewing_line_dimension] - 2
    before = lax.slice_in_dim(padded, 0, count, axis=viewing_line_dimension)
    after = lax.slice_in_dim(padded, 2, count + 2, axis=viewing_line_dimension)
    return (before - after) / (2.0 * mesh_cell_width)


def tendency(shifted, courant, heating):
    gradient = (
        45.0 * (shifted(1) - shifted(-1))
        - 9.0 * (shifted(2) - shifted(-2))
        + (shifted(3) - shifted(-3))
    ) / 60.0
    smoothing = (
        shifted(-3)
        + shifted(3)
        - 6.0 * (shifted(-2) + shifted(2))
        + 15.0 * (shifted(-1) + shifted(1))
        - 20.0 * shifted(0)
    )
    change_sum = FILTER_STRENGTH * smoothing - courant[None] * gradient
    return change_sum.at[0].add(COUPLING * heating)


def radiate(current, spectral_absorber_area, spectral_fraction_weight, mesh_cell_width):
    components, stations, row_count, col_count = current.shape
    line_data = jnp.transpose(current, (0, 2, 1, 3)).reshape(
        components, row_count, stations * col_count
    )
    gathered = lax.all_gather(line_data, "wall", axis=1, tiled=True)
    net_flux, wall_flux = viewing_line_irradiance(
        gathered[0],
        gathered[1:],
        spectral_absorber_area,
        spectral_fraction_weight,
        mesh_cell_width,
        1,
    )
    padded = edge_pad(net_flux, 0)
    row_start = lax.axis_index("wall") * row_count
    heating = divergence(
        lax.dynamic_slice_in_dim(padded, row_start, row_count + 2, 0), 0, mesh_cell_width
    )
    heating = jnp.transpose(heating.reshape(row_count, stations, col_count), (1, 0, 2))
    return (heating, wall_flux.reshape(stations, col_count))


def local(state, courant, cross_sections, band_fractions, absorb_index, band_index):
    spectral_absorber_area, spectral_fraction_weight = band_tables(
        absorb_index, band_index, cross_sections, band_fractions
    )
    mesh_cell_width = 1.0 / (state.shape[2] * lax.axis_size("wall"))
    col_count = state.shape[3]

    def segment_change(current):
        heating, wall_flux = radiate(
            current, spectral_absorber_area, spectral_fraction_weight, mesh_cell_width
        )
        padded = with_halo(current, (("azim", 3),), 3)

        def shifted(offset):
            return lax.slice_in_dim(padded, 3 + offset, 3 + offset + col_count, axis=3)

        return (tendency(shifted, courant, heating), wall_flux)

    first_change, first_flux = segment_change(state)
    middle = state + first_change
    second_change, second_flux = segment_change(middle)
    new_state = 0.5 * (state + middle + second_change)
    return (new_state, 0.5 * (first_flux + second_flux))


def solution(mesh):
    return jax.shard_map(
        local,
        mesh=mesh,
        in_specs=(P(None, "case", "wall", "azim"), P("case", "wall", "azim"), P(), P(), P(), P()),
        out_specs=(P(None, "case", "wall", "azim"), P("case", "azim")),
        check_vma=False,
    )
```

profile of v0, /device:TPU:0, one launch (start us, length us, event | category | flops | bytes accessed | tf_op | source)
XLA Modules:
  0.0 42.3 jit_solution(989441874617617582)
XLA Ops:
  0.6 1.0 %fusion.71 = (f32[12,1,8,3]{3,2,1,0:T(8,128)S(1)}, f32[12,1,8,3]{3,2,1,0:T(8,128)S(1)}) fusion(f32[12,1,8,128]{3,2,1,0:T(8,128)} %param.10), kind=kLoop, calls=%fused_computation.127 | loop fusion | bytes 4608 | tf_op jit(solution)/shard_map/slice | solution.py:21
  1.6 2.4 %collective-permute-start.1 = (f32[12,1,8,3]{3,2,1,0:T(8,128)S(1)}, f32[12,1,8,3]{3,2,1,0:T(8,128)S(1)}, u32[]{:S(2)}, u32[]{:S(2)}) collective-permute-start(f32[12,1,8,3]{3,2,1,0:T(8,128)S(1)} %get-tuple-element.34), channel_id=1, source_target_pairs={{1,0},{2,1},{3,2},{0,3},{5,4},{6,5},{7,6},{4,7},{9,8},{10,9},{11,1... | collective-permute-start | bytes 3464 | tf_op jit(solution)/shard_map/ppermute | solution.py:21
  4.1 14.1 %all-gather = f32[12,1,32,128]{3,1,0,2:T(1,128)S(1)} all-gather(f32[12,1,8,128]{3,1,0,2:T(1,128)S(1)} %copy.53), channel_id=2, replica_groups=mesh['case'=2,'wall'=4,'azim'=4] {'wall'}, dimensions={2}, use_global_device_ids=true | all-gather | bytes 245760 | tf_op jit(solution)/shard_map/all_gather | solution.py:110
  18.3 0.6 %copy-done.1 = s32[11,16]{1,0:T(8,128)S(1)} copy-done((s32[11,16]{1,0:T(8,128)S(1)}, s32[11,16]{1,0:T(8,128)}, u32[]{:S(2)}) %copy-start.1) | copy-done | bytes 728
  19.1 0.4 fusion.5
  19.6 0.6 %copy-done.4 = f32[64]{0:T(128)S(1)} copy-done((f32[64]{0:T(128)S(1)}, f32[64]{0:T(128)}, u32[]{:S(2)}) %copy-start.4) | copy-done | bytes 280
  20.2 0.2 select_reduce_fusion.1
  20.4 0.2 fusion.16
  20.7 0.2 fusion.21
  20.9 0.2 fusion.74
  21.1 0.2 fusion.75
  21.4 0.7 %copy-done.2 = f32[1,8,128]{2,1,0:T(8,128)S(1)} copy-done((f32[1,8,128]{2,1,0:T(8,128)S(1)}, f32[1,8,128]{2,1,0:T(8,128)}, u32[]{:S(2)}) %copy-start.2) | copy-done | bytes 4120
  22.5 13.8 %all-gather.1 = f32[12,1,32,128]{3,1,0,2:T(1,128)S(1)} all-gather(f32[12,1,8,128]{3,1,0,2:T(1,128)S(1)} %copy.56), channel_id=3, replica_groups=mesh['case'=2,'wall'=4,'azim'=4] {'wall'}, dimensions={2}, use_global_device_ids=true | all-gather | bytes 245760 | tf_op jit(solution)/shard_map/all_gather | solution.py:110
  36.4 0.4 fusion.4
  36.8 0.2 fusion.6
  37.1 0.2 fusion.11
  37.3 0.2 fusion.76
  37.6 0.2 fusion.77
  37.9 0.5 %collective-permute-start.2 = (f32[12,1,8,3]{3,2,1,0:T(8,128)S(1)}, f32[12,1,8,3]{3,2,1,0:T(8,128)S(1)}, u32[]{:S(2)}, u32[]{:S(2)}) collective-permute-start(f32[12,1,8,3]{3,2,1,0:T(8,128)S(1)} %get-tuple-element.33), channel_id=1, source_target_pairs={{0,1},{1,2},{2,3},{3,0},{4,5},{5,6},{6,7},{7,4},{8,9},{9,10},{10,1... | collective-permute-start | bytes 3464 | tf_op jit(solution)/shard_map/ppermute | solution.py:18
  38.4 0.5 %multiply_bitcast_fusion.1 = f32[1,128]{1,0:T(1,128)} fusion(f32[128]{0:T(128)S(1)} %get-tuple-element.40, f32[128]{0:T(128)S(1)} %get-tuple-element.41, f32[128]{0:T(128)S(1)} %get-tuple-element.42, f32[128]{0:T(128)S(1)} %get-tuple-element.43), kind=kLoop, calls=%fused_computation.115 | loop fusion | flops 1024 | bytes 2560 | tf_op jit(solution)/shard_map/mul | solution.py:150
  38.9 0.7 %collective-permute-done.3 = f32[12,1,8,3]{3,2,1,0:T(8,128)S(1)} collective-permute-done((f32[12,1,8,3]{3,2,1,0:T(8,128)S(1)}, f32[12,1,8,3]{3,2,1,0:T(8,128)S(1)}, u32[]{:S(2)}, u32[]{:S(2)}) %collective-permute-start.3) | collective-permute-done | bytes 1184 | tf_op jit(solution)/shard_map/ppermute | solution.py:21
  39.7 1.8 %collective-permute-done.2 = f32[12,1,8,3]{3,2,1,0:T(8,128)S(1)} collective-permute-done((f32[12,1,8,3]{3,2,1,0:T(8,128)S(1)}, f32[12,1,8,3]{3,2,1,0:T(8,128)S(1)}, u32[]{:S(2)}, u32[]{:S(2)}) %collective-permute-start.2) | collective-permute-done | bytes 1184 | tf_op jit(solution)/shard_map/ppermute | solution.py:18
  41.5 0.2 multiply_subtract_fusion
  41.7 0.6 %add_multiply_fusion = f32[12,1,8,128]{3,2,1,0:T(8,128)} fusion(f32[12,1,8,128]{3,2,1,0:T(8,128)S(1)} %fusion.55, f32[12,1,8,128]{3,2,1,0:T(8,128)S(1)} %copy-done, f32[12,1,8,128]{3,2,1,0:T(8,128)S(1)} %add.105), kind=kLoop, calls=%fused_computation.75 | loop fusion | flops 36864 | bytes 196608 | tf_op jit(solution)/shard_map/mul | solution.py:149
  (38 shorter events, 1.0 us)
Async XLA Ops:
  0.6 3.4 %copy-start = (f32[12,1,8,128]{3,2,1,0:T(8,128)S(1)}, f32[12,1,8,128]{3,2,1,0:T(8,128)}, u32[]{:S(2)}) copy-start(f32[12,1,8,128]{3,2,1,0:T(8,128)} %param.10) | copy-start | bytes 147460
  1.6 20.5 %collective-permute-start.1 = (f32[12,1,8,3]{3,2,1,0:T(8,128)S(1)}, f32[12,1,8,3]{3,2,1,0:T(8,128)S(1)}, u32[]{:S(2)}, u32[]{:S(2)}) collective-permute-start(f32[12,1,8,3]{3,2,1,0:T(8,128)S(1)} %get-tuple-element.34), channel_id=1, source_target_pairs={{1,0},{2,1},{3,2},{0,3},{5,4},{6,5},{7,6},{4,7},{9,8},{10,9},{11,1... | collective-permute-start | bytes 3464 | tf_op jit(solution)/shard_map/ppermute | solution.py:21
  4.0 18.2 %collective-permute-start = (f32[12,1,8,3]{3,2,1,0:T(8,128)S(1)}, f32[12,1,8,3]{3,2,1,0:T(8,128)S(1)}, u32[]{:S(2)}, u32[]{:S(2)}) collective-permute-start(f32[12,1,8,3]{3,2,1,0:T(8,128)S(1)} %get-tuple-element.35), channel_id=1, source_target_pairs={{0,1},{1,2},{2,3},{3,0},{4,5},{5,6},{6,7},{7,4},{8,9},{9,10},{10,1... | collective-permute-start | bytes 3464 | tf_op jit(solution)/shard_map/ppermute | solution.py:18
  18.2 0.7 %copy-start.1 = (s32[11,16]{1,0:T(8,128)S(1)}, s32[11,16]{1,0:T(8,128)}, u32[]{:S(2)}) copy-start(s32[11,16]{1,0:T(8,128)} %param.14) | copy-start | bytes 2116
  18.2 0.7 %copy-start.3 = (f32[64]{0:T(128)S(1)}, f32[64]{0:T(128)}, u32[]{:S(2)}) copy-start(f32[64]{0:T(128)} %param.12) | copy-start | bytes 772
  19.5 0.7 %copy-start.4 = (f32[64]{0:T(128)S(1)}, f32[64]{0:T(128)}, u32[]{:S(2)}) copy-start(f32[64]{0:T(128)} %param.13) | copy-start | bytes 772
  19.6 0.7 %copy-start.5 = (s32[16]{0:T(128)S(1)}, s32[16]{0:T(128)}, u32[]{:S(2)}) copy-start(s32[16]{0:T(128)} %param.15) | copy-start | bytes 196
  21.4 0.7 %copy-start.2 = (f32[1,8,128]{2,1,0:T(8,128)S(1)}, f32[1,8,128]{2,1,0:T(8,128)}, u32[]{:S(2)}) copy-start(f32[1,8,128]{2,1,0:T(8,128)} %param.11) | copy-start | bytes 12292
  37.8 1.8 %collective-permute-start.3 = (f32[12,1,8,3]{3,2,1,0:T(8,128)S(1)}, f32[12,1,8,3]{3,2,1,0:T(8,128)S(1)}, u32[]{:S(2)}, u32[]{:S(2)}) collective-permute-start(f32[12,1,8,3]{3,2,1,0:T(8,128)S(1)} %get-tuple-element.32), channel_id=1, source_target_pairs={{1,0},{2,1},{3,2},{0,3},{5,4},{6,5},{7,6},{4,7},{9,8},{10,9},{11,1... | collective-permute-start | bytes 3464 | tf_op jit(solution)/shard_map/ppermute | solution.py:21
  37.9 3.6 %collective-permute-start.2 = (f32[12,1,8,3]{3,2,1,0:T(8,128)S(1)}, f32[12,1,8,3]{3,2,1,0:T(8,128)S(1)}, u32[]{:S(2)}, u32[]{:S(2)}) collective-permute-start(f32[12,1,8,3]{3,2,1,0:T(8,128)S(1)} %get-tuple-element.33), channel_id=1, source_target_pairs={{0,1},{1,2},{2,3},{3,0},{4,5},{5,6},{6,7},{7,4},{8,9},{9,10},{10,1... | collective-permute-start | bytes 3464 | tf_op jit(solution)/shard_map/ppermute | solution.py:18
where the time goes:
time: 42.6 us; the launch traced here: 42.3 us
  blocking collectives  27.9 us (65%)
  other arithmetic  4.04 us (9%)
  local copies, waits for them, and re-layouts  3.18 us (7%)
  starting transfers between devices  2.94 us (7%)
  waiting for transfers between devices  2.52 us (6%)
  between operations  0.89 us (2%)
  matrix products  0.84 us (2%)
    all_gather x2, blocking collectives, radiate(): gathered = lax.all_gather(line_data, 'wall', axis=1, tiled=True)  27.9 us
    ppermute x2, starting transfers between devices, with_halo(): lax.ppermute(lax.slice_in_dim(block, 0, width, axis=dim), axis, backward)  2.44 us
    unnamed x14, local copies, waits for them, and re-layouts  2 us
    ppermute x2, waiting for transfers between devices, with_halo(): lax.ppermute(lax.slice_in_dim(block, block.shape[dim] - width, None, axis...  1.79 us
    slice x2, local copies, waits for them, and re-layouts, with_halo(): lax.slice_in_dim(block, 0, width, axis=dim)  1.05 us
    another operation x6, other arithmetic, viewing_line_irradiance(): lax.cumsum(optical_thickness_step, viewing_line_dimension)  1.01 us
    another operation x4, other arithmetic, viewing_line_irradiance(): lax.cumsum(radiated_energy_rate * falloff, viewing_line_dimension, revers...  0.98 us
  transfers between devices with their start and end apart: 4, of which 2 were waited for; matrix products, arithmetic and copies ran while one was open for 6% of the time, Pallas kernels for 0%

commit v1 on v0

--- a/solution.py
+++ b/solution.py
@@ -7,6 +7,19 @@
 KERNEL_RATES = (1.15, 3.4)
 FILTER_STRENGTH = 0.02
 COUPLING = 0.1
+
+
+def ring_gather(value, axis, dim):
+    ways = lax.axis_size(axis)
+    up = [(d, (d + 1) % ways) for d in range(ways)]
+    down = [(d, (d - 1) % ways) for d in range(ways)]
+    earlier, later = ([value], [value])
+    for _ in range(ways // 2):
+        earlier.append(lax.ppermute(earlier[-1], axis, up))
+    for _ in range((ways - 1) // 2):
+        later.append(lax.ppermute(later[-1], axis, down))
+    line = jnp.concatenate([*earlier[::-1], *later[1:]], axis=dim)
+    return jnp.roll(line, (lax.axis_index(axis) - ways // 2) * value.shape[dim], axis=dim)
 
 
 def with_halo(block, sides, width):
@@ -107,7 +120,7 @@
     line_data = jnp.transpose(current, (0, 2, 1, 3)).reshape(
         components, row_count, stations * col_count
     )
-    gathered = lax.all_gather(line_data, "wall", axis=1, tiled=True)
+    gathered = ring_gather(line_data, "wall", 1)
     net_flux, wall_flux = viewing_line_irradiance(
         gathered[0],
         gathered[1:],

time: 42.6 us -> 35.7 us (0.84)
  blocking collectives: 27.9 us -> 0 us
  waiting for transfers between devices: 2.52 us -> 16.1 us
  starting transfers between devices: 2.94 us -> 10.1 us
  other arithmetic: 4.04 us -> 4.59 us
    all_gather x2 -> x0, blocking collectives: 27.9 us -> none  [radiate(): gathered = lax.all_gather(line_data, 'wall', axis=1, tiled=True)]
    ppermute x0 -> x6, waiting for transfers between devices: none -> 16.1 us  [the longest x4 15.8 us: ring_gather(): earlier.append(lax.ppermute(earlier[-1], axis, up))]
    ppermute x0 -> x6, starting transfers between devices: none -> 8.93 us  [the longest x2 8.92 us: ring_gather(): later.append(lax.ppermute(later[-1], axis, down))]
    ppermute x2, waiting for transfers between devices: 1.79 us -> 0.01 us  [with_halo(): lax.ppermute(lax.slice_in_dim(block, block.shape[dim] - width, None, axis...]
    ppermute x2, starting transfers between devices: 2.44 us -> 0.71 us  [with_halo(): lax.ppermute(lax.slice_in_dim(block, 0, width, axis=dim), axis, backward)]
    slice x2, local copies, waits for them, and re-layouts: 1.05 us -> 0.15 us  [with_halo(): lax.slice_in_dim(block, 0, width, axis=dim)]
    ppermute x2, waiting for transfers between devices: 0.73 us -> 0.01 us  [with_halo(): lax.ppermute(lax.slice_in_dim(block, 0, width, axis=dim), axis, backward)]
    unnamed x14, local copies, waits for them, and re-layouts: 2 us -> 2.69 us
  transfers between devices with their start and end apart: 4 -> 10, of which waited for: 2 -> 5; matrix products, arithmetic and copies ran while one was open for 6% -> 2% of each run, Pallas kernels for 0% -> 0%
where the time goes in v1:
time: 35.7 us; the launch traced here: 35.5 us
  waiting for transfers between devices  16.1 us (45%)
  starting transfers between devices  10.1 us (28%)
  other arithmetic  4.59 us (13%)
  local copies, waits for them, and re-layouts  2.87 us (8%)
  between operations  0.92 us (3%)
  matrix products  0.87 us (2%)
    ppermute x4, waiting for transfers between devices, ring_gather(): earlier.append(lax.ppermute(earlier[-1], axis, up))  15.8 us
    ppermute x2, starting transfers between devices, ring_gather(): later.append(lax.ppermute(later[-1], axis, down))  8.92 us
    unnamed x14, local copies, waits for them, and re-layouts  2.69 us
    another operation x6, other arithmetic, viewing_line_irradiance(): lax.cumsum(optical_thickness_step, viewing_line_dimension)  1.01 us
    another operation x4, other arithmetic, viewing_line_irradiance(): lax.cumsum(radiated_energy_rate * falloff, viewing_line_dimension, revers...  0.98 us
    dot_general x2, matrix products, viewing_line_irradiance(): jnp.einsum('kb,kij->bij', spectral_absorber_area, species_concentrations,...  0.87 us
    ppermute x2, starting transfers between devices, with_halo(): lax.ppermute(lax.slice_in_dim(block, 0, width, axis=dim), axis, backward)  0.71 us
  transfers between devices with their start and end apart: 10, of which 5 were waited for; matrix products, arithmetic and copies ran while one was open for 2% of the time, Pallas kernels for 0%

profile of v1, /device:TPU:0, one launch (start us, length us, event | category | flops | bytes accessed | tf_op | source)
XLA Modules:
  0.0 35.5 jit_solution(6811547295277389589)
XLA Ops:
  0.6 0.9 %copy.47 = f32[12,1,8,128]{3,0,2,1:T(8,128)S(1)} copy(f32[12,1,8,128]{3,2,1,0:T(8,128)} %param.12) | data formatting | bytes 98304 | tf_op args[0]
  1.5 5.1 %collective-permute-start.4 = (f32[12,8,128]{2,0,1:T(8,128)S(1)}, f32[12,8,128]{2,0,1:T(8,128)S(1)}, u32[]{:S(2)}, u32[]{:S(2)}) collective-permute-start(f32[12,8,128]{2,0,1:T(8,128)S(1)} %bitcast.36), channel_id=1, source_target_pairs={{0,12},{4,0},{8,4},{12,8},{1,13},{5,1},{9,5},{13,9},{2,14},{6,2},{... | collective-permute-start | bytes 147464 | tf_op jit(solution)/shard_map/ppermute | solution.py:20
  6.7 0.7 %collective-permute-start.1 = (f32[12,1,8,3]{3,2,1,0:T(8,128)S(1)}, f32[12,1,8,3]{3,2,1,0:T(8,128)S(1)}, u32[]{:S(2)}, u32[]{:S(2)}) collective-permute-start(f32[12,1,8,3]{3,2,1,0:T(8,128)S(1)} %get-tuple-element.33), channel_id=1, source_target_pairs={{1,0},{2,1},{3,2},{0,3},{5,4},{6,5},{7,6},{4,7},{9,8},{10,9},{11,1... | collective-permute-start | bytes 3464 | tf_op jit(solution)/shard_map/ppermute | solution.py:34
  7.4 0.7 %copy-done.2 = f32[1,8,128]{2,1,0:T(8,128)S(1)} copy-done((f32[1,8,128]{2,1,0:T(8,128)S(1)}, f32[1,8,128]{2,1,0:T(8,128)}, u32[]{:S(2)}) %copy-start.2) | copy-done | bytes 4120
  8.1 0.6 %copy-done.4 = f32[64]{0:T(128)S(1)} copy-done((f32[64]{0:T(128)S(1)}, f32[64]{0:T(128)}, u32[]{:S(2)}) %copy-start.4) | copy-done | bytes 280
  8.9 0.5 %copy-done.3 = f32[64]{0:T(128)S(1)} copy-done((f32[64]{0:T(128)S(1)}, f32[64]{0:T(128)}, u32[]{:S(2)}) %copy-start.3) | copy-done | bytes 280
  9.6 3.1 %collective-permute-done.2 = f32[12,8,128]{2,0,1:T(8,128)S(1)} collective-permute-done((f32[12,8,128]{2,0,1:T(8,128)S(1)}, f32[12,8,128]{2,0,1:T(8,128)S(1)}, u32[]{:S(2)}, u32[]{:S(2)}) %collective-permute-start.2) | collective-permute-done | bytes 49184 | tf_op jit(solution)/shard_map/ppermute | solution.py:18
  12.9 5.9 %collective-permute-done.3 = f32[12,8,128]{2,0,1:T(8,128)S(1)} collective-permute-done((f32[12,8,128]{2,0,1:T(8,128)S(1)}, f32[12,8,128]{2,0,1:T(8,128)S(1)}, u32[]{:S(2)}, u32[]{:S(2)}) %collective-permute-start.3) | collective-permute-done | bytes 49184 | tf_op jit(solution)/shard_map/ppermute | solution.py:18
  18.7 0.4 %fusion.7 = f32[12,32,128]{2,0,1:T(8,128)S(1)} fusion(s32[]{:T(128)S(6)} %select_n.28, f32[12,8,128]{2,0,1:T(8,128)S(1)} %collective-permute-done.3, f32[12,8,128]{2,0,1:T(8,128)S(1)} %collective-permute-done.2, f32[12,8,128]{2,0,1:T(8,128)S(1)} %bitcast.38, f32[12,8,128]{2,0,1:T(8,128)S(1)} %collective-permute-done.4), kind=kLoop, calls=%fused_computation.29 | loop fusion | flops 344064 | bytes 393220 | tf_op jit(solution)/shard_map/jit(_roll_dynamic)/concatenate | solution.py:22
  19.2 0.4 %fusion.11 = f32[16,32,128]{2,0,1:T(8,128)S(1)} fusion(f32[12,32,128]{2,0,1:T(8,128)S(1)} %fusion.7, f32[11,16]{1,0:T(8,128)S(1)} %select_reduce_fusion), kind=kOutput, calls=%fused_computation.33 | convolution fusion | flops 8650752 | bytes 459456 | tf_op jit(solution)/shard_map/kb,kij->bij/dot_general | solution.py:58
  19.7 0.2 fusion.25
  19.9 0.2 fusion.30
  20.2 0.2 fusion.89
  20.4 0.2 fusion.90
  20.9 0.5 %collective-permute-start.5 = (f32[12,1,8,3]{3,2,1,0:T(8,128)S(1)}, f32[12,1,8,3]{3,2,1,0:T(8,128)S(1)}, u32[]{:S(2)}, u32[]{:S(2)}) collective-permute-start(f32[12,1,8,3]{3,2,1,0:T(8,128)S(1)} %get-tuple-element.32), channel_id=1, source_target_pairs={{0,1},{1,2},{2,3},{3,0},{4,5},{5,6},{6,7},{7,4},{8,9},{9,10},{10,1... | collective-permute-start | bytes 3464 | tf_op jit(solution)/shard_map/ppermute | solution.py:31
  21.4 3.8 %collective-permute-start.9 = (f32[12,8,128]{2,1,0:T(8,128)S(1)}, f32[12,8,128]{2,1,0:T(8,128)S(1)}, u32[]{:S(2)}, u32[]{:S(2)}) collective-permute-start(f32[12,8,128]{2,1,0:T(8,128)S(1)} %bitcast.30), channel_id=1, source_target_pairs={{0,12},{4,0},{8,4},{12,8},{1,13},{5,1},{9,5},{13,9},{2,14},{6,2},{... | collective-permute-start | bytes 147464 | tf_op jit(solution)/shard_map/ppermute | solution.py:20
  25.2 1.5 %collective-permute-done.7 = f32[12,8,128]{2,1,0:T(8,128)S(1)} collective-permute-done((f32[12,8,128]{2,1,0:T(8,128)S(1)}, f32[12,8,128]{2,1,0:T(8,128)S(1)}, u32[]{:S(2)}, u32[]{:S(2)}) %collective-permute-start.7) | collective-permute-done | bytes 49184 | tf_op jit(solution)/shard_map/ppermute | solution.py:18
  27.0 0.3 collective-permute-done.9
  27.3 5.4 %collective-permute-done.8 = f32[12,8,128]{2,1,0:T(8,128)S(1)} collective-permute-done((f32[12,8,128]{2,1,0:T(8,128)S(1)}, f32[12,8,128]{2,1,0:T(8,128)S(1)}, u32[]{:S(2)}, u32[]{:S(2)}) %collective-permute-start.8) | collective-permute-done | bytes 49184 | tf_op jit(solution)/shard_map/ppermute | solution.py:18
  32.8 0.5 %fusion.13 = f32[16,32,128]{2,0,1:T(8,128)S(1)} fusion(f32[11,32,128]{2,1,0:T(8,128)S(1)} %slice.233, f32[11,16]{1,0:T(8,128)S(1)} %select_reduce_fusion), kind=kOutput, calls=%fused_computation.35 | convolution fusion | flops 8650752 | bytes 443072 | tf_op jit(solution)/shard_map/kb,kij->bij/dot_general | solution.py:58
  33.3 0.2 fusion.15
  33.5 0.2 fusion.20
  34.3 0.6 %add_multiply_fusion = f32[12,1,8,128]{3,2,1,0:T(8,128)} fusion(f32[12,1,8,128]{3,2,1,0:T(8,128)S(1)} %constant_dynamic-update-slice_fusion.2, f32[12,1,8,128]{3,2,1,0:T(8,128)S(1)} %copy-done, f32[12,1,8,128]{3,2,1,0:T(8,128)S(1)} %add.114), kind=kLoop, calls=%fused_computation.106 | loop fusion | flops 36864 | bytes 196608 | tf_op jit(solution)/shard_map/mul | solution.py:162
  35.0 0.5 %multiply_bitcast_fusion.1 = f32[1,128]{1,0:T(1,128)} fusion(f32[128]{0:T(128)S(1)} %get-tuple-element.39, f32[128]{0:T(128)S(1)} %get-tuple-element.40, f32[128]{0:T(128)S(1)} %get-tuple-element.41, f32[128]{0:T(128)S(1)} %get-tuple-element.42), kind=kLoop, calls=%fused_computation.147 | loop fusion | flops 1024 | bytes 2560 | tf_op jit(solution)/shard_map/mul | solution.py:163
  (48 shorter events, 1.9 us)
Async XLA Ops:
  0.6 6.0 %copy-start = (f32[12,1,8,128]{3,2,1,0:T(8,128)S(1)}, f32[12,1,8,128]{3,2,1,0:T(8,128)}, u32[]{:S(2)}) copy-start(f32[12,1,8,128]{3,2,1,0:T(8,128)} %param.12) | copy-start | bytes 147460
  1.5 11.4 %collective-permute-start.4 = (f32[12,8,128]{2,0,1:T(8,128)S(1)}, f32[12,8,128]{2,0,1:T(8,128)S(1)}, u32[]{:S(2)}, u32[]{:S(2)}) collective-permute-start(f32[12,8,128]{2,0,1:T(8,128)S(1)} %bitcast.36), channel_id=1, source_target_pairs={{0,12},{4,0},{8,4},{12,8},{1,13},{5,1},{9,5},{13,9},{2,14},{6,2},{... | collective-permute-start | bytes 147464 | tf_op jit(solution)/shard_map/ppermute | solution.py:20
  6.6 6.1 %collective-permute-start.2 = (f32[12,8,128]{2,0,1:T(8,128)S(1)}, f32[12,8,128]{2,0,1:T(8,128)S(1)}, u32[]{:S(2)}, u32[]{:S(2)}) collective-permute-start(f32[12,8,128]{2,0,1:T(8,128)S(1)} %bitcast.37), channel_id=1, source_target_pairs={{0,4},{4,8},{8,12},{12,0},{1,5},{5,9},{9,13},{13,1},{2,6},{6,10},{... | collective-permute-start | bytes 147464 | tf_op jit(solution)/shard_map/ppermute | solution.py:18
  6.7 2.9 %collective-permute-start.1 = (f32[12,1,8,3]{3,2,1,0:T(8,128)S(1)}, f32[12,1,8,3]{3,2,1,0:T(8,128)S(1)}, u32[]{:S(2)}, u32[]{:S(2)}) collective-permute-start(f32[12,1,8,3]{3,2,1,0:T(8,128)S(1)} %get-tuple-element.33), channel_id=1, source_target_pairs={{1,0},{2,1},{3,2},{0,3},{5,4},{6,5},{7,6},{4,7},{9,8},{10,9},{11,1... | collective-permute-start | bytes 3464 | tf_op jit(solution)/shard_map/ppermute | solution.py:34
  7.4 5.3 %collective-permute-start = (f32[12,1,8,3]{3,2,1,0:T(8,128)S(1)}, f32[12,1,8,3]{3,2,1,0:T(8,128)S(1)}, u32[]{:S(2)}, u32[]{:S(2)}) collective-permute-start(f32[12,1,8,3]{3,2,1,0:T(8,128)S(1)} %get-tuple-element.34), channel_id=1, source_target_pairs={{0,1},{1,2},{2,3},{3,0},{4,5},{5,6},{6,7},{7,4},{8,9},{9,10},{10,1... | collective-permute-start | bytes 3464 | tf_op jit(solution)/shard_map/ppermute | solution.py:31
  7.4 0.7 %copy-start.2 = (f32[1,8,128]{2,1,0:T(8,128)S(1)}, f32[1,8,128]{2,1,0:T(8,128)}, u32[]{:S(2)}) copy-start(f32[1,8,128]{2,1,0:T(8,128)} %param.13) | copy-start | bytes 12292
  7.4 1.5 %copy-start.1 = (s32[11,16]{1,0:T(8,128)S(1)}, s32[11,16]{1,0:T(8,128)}, u32[]{:S(2)}) copy-start(s32[11,16]{1,0:T(8,128)} %param.16) | copy-start | bytes 2116
  8.1 0.7 %copy-start.4 = (f32[64]{0:T(128)S(1)}, f32[64]{0:T(128)}, u32[]{:S(2)}) copy-start(f32[64]{0:T(128)} %param.15) | copy-start | bytes 772
  8.1 0.7 %copy-start.5 = (s32[16]{0:T(128)S(1)}, s32[16]{0:T(128)}, u32[]{:S(2)}) copy-start(s32[16]{0:T(128)} %param.17) | copy-start | bytes 196
  8.7 0.7 %copy-start.3 = (f32[64]{0:T(128)S(1)}, f32[64]{0:T(128)}, u32[]{:S(2)}) copy-start(f32[64]{0:T(128)} %param.14) | copy-start | bytes 772
  12.7 6.1 %collective-permute-start.3 = (f32[12,8,128]{2,0,1:T(8,128)S(1)}, f32[12,8,128]{2,0,1:T(8,128)S(1)}, u32[]{:S(2)}, u32[]{:S(2)}) collective-permute-start(f32[12,8,128]{2,0,1:T(8,128)S(1)} %collective-permute-done.2), channel_id=1, source_target_pairs={{0,4},{4,8},{8,12},{12,0},{1,5},{5,9},{9,13},{13,1},{2,6},{6,10},{... | collective-permute-start | bytes 147464 | tf_op jit(solution)/shard_map/ppermute | solution.py:18
  20.8 5.9 %collective-permute-start.7 = (f32[12,8,128]{2,1,0:T(8,128)S(1)}, f32[12,8,128]{2,1,0:T(8,128)S(1)}, u32[]{:S(2)}, u32[]{:S(2)}) collective-permute-start(f32[12,8,128]{2,1,0:T(8,128)S(1)} %bitcast.29), channel_id=1, source_target_pairs={{0,4},{4,8},{8,12},{12,0},{1,5},{5,9},{9,13},{13,1},{2,6},{6,10},{... | collective-permute-start | bytes 147464 | tf_op jit(solution)/shard_map/ppermute | solution.py:18
  20.9 5.9 %collective-permute-start.6 = (f32[12,1,8,3]{3,2,1,0:T(8,128)S(1)}, f32[12,1,8,3]{3,2,1,0:T(8,128)S(1)}, u32[]{:S(2)}, u32[]{:S(2)}) collective-permute-start(f32[12,1,8,3]{3,2,1,0:T(8,128)S(1)} %get-tuple-element.31), channel_id=1, source_target_pairs={{1,0},{2,1},{3,2},{0,3},{5,4},{6,5},{7,6},{4,7},{9,8},{10,9},{11,1... | collective-permute-start | bytes 3464 | tf_op jit(solution)/shard_map/ppermute | solution.py:34
  20.9 5.8 %collective-permute-start.5 = (f32[12,1,8,3]{3,2,1,0:T(8,128)S(1)}, f32[12,1,8,3]{3,2,1,0:T(8,128)S(1)}, u32[]{:S(2)}, u32[]{:S(2)}) collective-permute-start(f32[12,1,8,3]{3,2,1,0:T(8,128)S(1)} %get-tuple-element.32), channel_id=1, source_target_pairs={{0,1},{1,2},{2,3},{3,0},{4,5},{5,6},{6,7},{7,4},{8,9},{9,10},{10,1... | collective-permute-start | bytes 3464 | tf_op jit(solution)/shard_map/ppermute | solution.py:31
  21.4 5.8 %collective-permute-start.9 = (f32[12,8,128]{2,1,0:T(8,128)S(1)}, f32[12,8,128]{2,1,0:T(8,128)S(1)}, u32[]{:S(2)}, u32[]{:S(2)}) collective-permute-start(f32[12,8,128]{2,1,0:T(8,128)S(1)} %bitcast.30), channel_id=1, source_target_pairs={{0,12},{4,0},{8,4},{12,8},{1,13},{5,1},{9,5},{13,9},{2,14},{6,2},{... | collective-permute-start | bytes 147464 | tf_op jit(solution)/shard_map/ppermute | solution.py:20
  26.7 5.9 %collective-permute-start.8 = (f32[12,8,128]{2,1,0:T(8,128)S(1)}, f32[12,8,128]{2,1,0:T(8,128)S(1)}, u32[]{:S(2)}, u32[]{:S(2)}) collective-permute-start(f32[12,8,128]{2,1,0:T(8,128)S(1)} %collective-permute-done.7), channel_id=1, source_target_pairs={{0,4},{4,8},{8,12},{12,0},{1,5},{5,9},{9,13},{13,1},{2,6},{6,10},{... | collective-permute-start | bytes 147464 | tf_op jit(solution)/shard_map/ppermute | solution.py:18
